TPU v7x, 512 devices: a whole 4x8x8 slice. The times are simulated.
512 devices in a mesh: seq: 32 (over z, x), dp: 2 (over core), tensor: 8 (over y).
Axes of the slice: x: 4, y: 8, z: 8, core: 2. Of those that a mesh axis runs over, the one named last changes fastest.
Arguments:
- head_inputs: bfloat16 [2, 2560, 16384], P('dp', 'tensor', 'seq'), may hold values from -6 to 6
- b_proj: bfloat16 [2, 16384, 128], P('dp', 'seq'), may hold values from -0.59765625 to 0.59765625
- c_proj: bfloat16 [2, 16384, 128], P('dp', 'seq'), may hold values from -0.59765625 to 0.59765625
- dt_raw: float32 [2, 40, 16384], P('dp', 'tensor', 'seq'), may hold values from -2 to 0
- a_log: float32 [40], P('tensor'), as said below
- d_skip: float32 [40], P('tensor'), may hold values from 0.5 to 1.5
- w_out: bfloat16 [2560, 2560], P('tensor', 'dp'), may hold values from -0.125 to 0.125
- out_grad: bfloat16 [2, 2560, 16384], P('dp', 'tensor', 'seq'), may hold values from -6 to 6
Outputs:
- mixed: bfloat16 [2, 2560, 16384], P('dp', 'tensor', 'seq')
- grad_inputs: bfloat16 [2, 2560, 16384], P('dp', 'tensor', 'seq')
- grad_b: bfloat16 [2, 16384, 128], P('dp', 'seq')
- grad_c: bfloat16 [2, 16384, 128], P('dp', 'seq')
- grad_dt: float32 [2, 40, 16384], P('dp', 'tensor', 'seq')
- grad_alog: float32 [40], P('tensor')
- grad_skip: float32 [40], P('tensor')
- grad_w: bfloat16 [2560, 2560], P('tensor', ('seq', 'dp'))
Inputs may be any that keep to these rules, and one draw needn't show every extreme that they name: exp(a_log) lies between 0.1 / 16384 and 0.1.
All inputs are finite; a program needn't handle non-finite values.
Results may differ from a plain program's by a relative error of at most 0.0049.
Values may be sent and summed in bfloat16 or wider, within the bound.
A program may use at most 128 MiB of HBM per device.

v0:
```python
import jax
import jax.numpy as jnp
from jax import lax
from jax.sharding import PartitionSpec as P

SPAN = 256
HIGH = lax.Precision.HIGHEST


def span_pass(carried, x_block, b_block, c_block, step_block, decay_rate):
    log_decay = step_block * decay_rate[:, None]
    cumulative = jnp.cumsum(log_decay, axis=1)
    block = cumulative.shape[1]
    indices = jnp.arange(block)
    causal = (indices[:, None] >= indices[None, :])[None, :, :]
    spread = cumulative[:, :, None] - cumulative[:, None, :]
    weights = jnp.where(causal, jnp.exp(jnp.where(causal, spread, 0.0)), 0.0)
    affinity = jnp.dot(c_block, b_block.T, precision=HIGH)
    scores = affinity[None, :, :] * weights * step_block[:, None, :]
    block_out = jnp.einsum("hps,hts->hpt", x_block, scores, precision=HIGH)
    block_out = block_out + jnp.exp(cumulative)[:, None, :] * jnp.einsum(
        "hpn,tn->hpt", carried, c_block, precision=HIGH
    )
    tail_weight = jnp.exp(cumulative[:, -1:] - cumulative) * step_block
    updated = jnp.exp(cumulative[:, -1])[:, None, None] * carried
    updated = updated + jnp.einsum(
        "hps,sn->hpn", x_block * tail_weight[:, None, :], b_block, precision=HIGH
    )
    return (updated, block_out)


def sweep(streams, b_rows, c_rows, dt_rows, alog_part, skip_part, state_in):
    head_count, head_width, length = streams.shape
    blocks = length // SPAN
    step_size = jax.nn.softplus(dt_rows)
    decay_rate = -jnp.exp(alog_part)
    x_blocks = streams.reshape(head_count, head_width, blocks, SPAN).transpose(2, 0, 1, 3)
    b_blocks = b_rows.reshape(blocks, SPAN, b_rows.shape[1])
    c_blocks = c_rows.reshape(blocks, SPAN, c_rows.shape[1])
    s_blocks = step_size.reshape(head_count, blocks, SPAN).transpose(1, 0, 2)

    def advance(carried, inputs):
        return span_pass(carried, inputs[0], inputs[1], inputs[2], inputs[3], decay_rate)

    state_end, outputs = lax.scan(advance, state_in, (x_blocks, b_blocks, c_blocks, s_blocks))
    mixed_f = outputs.transpose(1, 2, 0, 3).reshape(head_count, head_width, length)
    return (mixed_f + skip_part[:, None, None] * streams, state_end)


def per_device(head_inputs, b_proj, c_proj, dt_raw, a_log, d_skip, w_out, out_grad):
    head_count = dt_raw.shape[1]
    length = head_inputs.shape[2]
    head_width = head_inputs.shape[1] // head_count
    streams = head_inputs[0].astype(jnp.float32).reshape(head_count, head_width, length)
    b_rows = b_proj[0].astype(jnp.float32)
    c_rows = c_proj[0].astype(jnp.float32)
    dt_rows = dt_raw[0]
    decay_rate = -jnp.exp(a_log)
    step_size = jax.nn.softplus(dt_rows)
    cumulative = jnp.cumsum(step_size * decay_rate[:, None], axis=1)
    device_decay = cumulative[:, -1]
    tail_weight = jnp.exp(device_decay[:, None] - cumulative) * step_size
    local_state = jnp.einsum(
        "hpt,tn->hpn", streams * tail_weight[:, None, :], b_rows, precision=HIGH
    )
    totals = lax.all_gather(device_decay[None, :], "seq", axis=0, tiled=True)
    prefix = jnp.cumsum(totals, axis=0)
    my_index = lax.axis_index("seq")
    reached = lax.dynamic_index_in_dim(prefix, my_index, 0, keepdims=False)
    before = reached - device_decay
    shard_part = lax.all_gather(local_state[None], "seq", axis=0, tiled=True)
    row_count = shard_part.shape[0]
    indices = jnp.arange(row_count, dtype=jnp.int32)
    prefix_ends = prefix
    active = (indices < my_index)[:, None]
    weights = jnp.where(active, jnp.exp(jnp.where(active, before[None, :] - prefix_ends, 0.0)), 0.0)
    state_in = jnp.einsum("jh,jhpn->hpn", weights, shard_part, precision=HIGH)

    def local_sweep(xa, ba, ca, da, aa, sa):
        return sweep(xa, ba, ca, da, aa, sa, state_in)

    primal, pullback = jax.vjp(local_sweep, streams, b_rows, c_rows, dt_rows, a_log, d_skip)
    mixed_half = primal[0].reshape(head_count * head_width, length).astype(jnp.bfloat16)
    g_full = lax.all_gather(out_grad[0], "tensor", axis=0, tiled=True)
    cotan_sum = jnp.dot(
        lax.all_gather(w_out, "dp", axis=1, tiled=True), g_full, preferred_element_type=jnp.float32
    )
    cotan_half = cotan_sum.astype(jnp.bfloat16)
    y_cotan = (
        lax.optimization_barrier(cotan_half)
        .astype(jnp.float32)
        .reshape(head_count, head_width, length)
    )
    local_cotan = jnp.einsum(
        "hpt,tn->hpn", y_cotan * jnp.exp(cumulative)[:, None, :], c_rows, precision=HIGH
    )
    shard_part = lax.all_gather(local_cotan[None], "seq", axis=0, tiled=True)
    row_count = shard_part.shape[0]
    indices = jnp.arange(row_count, dtype=jnp.int32)
    prefix_ends = prefix
    active = (indices > my_index)[:, None]
    weights = jnp.where(
        active, jnp.exp(jnp.where(active, prefix_ends - totals - reached[None, :], 0.0)), 0.0
    )
    cotan_in = jnp.einsum("jh,jhpn->hpn", weights, shard_part, precision=HIGH)
    grads = pullback((y_cotan, cotan_in))
    w_terms = lax.dot_general(
        mixed_half, g_full, (((1,), (1,)), ((), ())), preferred_element_type=jnp.float32
    )
    grad_w = lax.psum_scatter(w_terms, ("seq", "dp"), scatter_dimension=1, tiled=True).astype(
        jnp.bfloat16
    )
    grad_b, grad_c = lax.psum((grads[1], grads[2]), "tensor")
    grad_alog, grad_skip = lax.psum((grads[4], grads[5]), ("seq", "dp"))
    grad_inputs = grads[0].reshape(head_count * head_width, length).astype(jnp.bfloat16)
    return (
        mixed_half[None],
        grad_inputs[None],
        grad_b.astype(jnp.bfloat16)[None],
        grad_c.astype(jnp.bfloat16)[None],
        grads[3][None],
        grad_alog,
        grad_skip,
        grad_w,
    )


def solution(mesh):
    in_specs = (
        P("dp", "tensor", "seq"),
        P("dp", "seq", None),
        P("dp", "seq", None),
        P("dp", "tensor", "seq"),
        P("tensor"),
        P("tensor"),
        P("tensor", "dp"),
        P("dp", "tensor", "seq"),
    )
    out_specs = (
        P("dp", "tensor", "seq"),
        P("dp", "tensor", "seq"),
        P("dp", "seq", None),
        P("dp", "seq", None),
        P("dp", "tensor", "seq"),
        P("tensor"),
        P("tensor"),
        P("tensor", ("seq", "dp")),
    )
    return jax.shard_map(
        per_device, mesh=mesh, in_specs=in_specs, out_specs=out_specs, check_vma=False
    )
```

profile of v0, /device:TPU:16, one launch (start us, length us, event | category | flops | bytes accessed | tf_op | source)
XLA Modules:
  0.0 658.8 jit_solution(519363650831749236)
XLA Ops:
  15.4 17.3 %all-gather.9.cloned.1.call-done = bf16[320,2560]{1,0:T(8,128)(2,1)} async-done(((bf16[320,1280]{1,0:T(8,128)(2,1)}), bf16[320,2560]{1,0:T(8,128)(2,1)}) %all-gather.9.cloned.1.call-update) | async-done | bytes 1638416 | tf_op jit(solution)/shard_map/all_gather | solution.py:86
  32.7 47.4 %all-gather.13.cloned.1.call-done = bf16[1,2560,512]{2,1,0:T(8,128)(2,1)} async-done(((bf16[1,320,512]{2,1,0:T(8,128)(2,1)}), bf16[1,2560,512]{2,1,0:T(8,128)(2,1)}) %all-gather.13.cloned.1.call-update) | async-done | bytes 2621456 | tf_op jit(solution)/shard_map/all_gather | solution.py:84
  80.0 3.2 fusion.131
  87.3 76.9 %all-reduce.2 = f32[160]{0:T(256)S(1)} all-reduce(f32[160]{0:T(256)S(1)} %dynamic-update-slice), channel_id=2, replica_groups=mesh['seq'=32,'dp'=2,'tensor'=8] {'seq'}, use_global_device_ids=true, to_apply=%add.2 | all-reduce | flops 160 | bytes 1280
  167.5 7.2 %all-gather.11.cloned.1.call-done = f32[160,64,128]{2,1,0:T(8,128)} async-done(((f32[5,64,128]{2,1,0:T(8,128)}), f32[160,64,128]{2,1,0:T(8,128)}) %all-gather.11.cloned.1.call-update) | async-done | bytes 5242896 | tf_op jit(solution)/shard_map/all_gather | solution.py:71
  174.6 7.7 %fusion.125 = f32[5,1,64,128]{3,1,2,0:T(1,128)S(1)} fusion(f32[32,5,1,1]{0,2,3,1:T(1,128)S(1)} %copy.117, f32[32,5,64,128]{3,2,1,0:T(8,128)} %bitcast.487), kind=kOutput, calls=%fused_computation.159 | convolution fusion | flops 15728640 | bytes 5407360 | tf_op jit(solution)/shard_map/jh,jhpn->hpn/dot_general | solution.py:77
  185.1 23.1 %while.75 = (s32[]{:T(128)}, f32[5,64,128]{2,1,0:T(8,128)S(1)}, f32[2,5,64,256]{3,2,1,0:T(8,128)}, f32[2,5,256,256]{3,2,1,0:T(8,128)}, f32[2,128,256]{1,2,0:T(8,...) while((s32[]{:T(128)}, f32[5,64,128]{2,1,0:T(8,128)S(1)}, ...), condition=%wide.region_6.7_spmd.clone.clone, body=%wide.region_3.6_spmd.clone.clone.sunk | while | flops 607838976 | bytes 16159797 | solution.py:45
  188.2 2.8 multiply_dynamic-update-slice_fusion.4
  192.4 2.4 fusion.212
  199.8 2.8 multiply_dynamic-update-slice_fusion.4
  204.0 2.4 fusion.212
  211.3 5.4 fusion.127
  217.6 48.0 %all-gather.15.cloned.1.call-done = f32[160,64,128]{2,1,0:T(8,128)} async-done(((f32[5,64,128]{2,1,0:T(8,128)}), f32[160,64,128]{2,1,0:T(8,128)}) %all-gather.15.cloned.1.call-update) | async-done | bytes 5242896 | tf_op jit(solution)/shard_map/all_gather | solution.py:97
  265.6 7.7 %fusion.123 = f32[5,1,64,128]{3,1,2,0:T(1,128)S(1)} fusion(f32[32,5,1,1]{0,2,3,1:T(1,128)S(1)} %copy.120, f32[32,5,64,128]{3,2,1,0:T(8,128)} %bitcast.486), kind=kOutput, calls=%fused_computation.157 | convolution fusion | flops 15728640 | bytes 5407360 | tf_op jit(solution)/shard_map/jh,jhpn->hpn/dot_general | solution.py:105
  275.7 46.3 %while.76 = (s32[]{:T(128)}, f32[5]{0:T(128)S(1)}, f32[5,64,128]{2,1,0:T(8,128)S(1)}, f32[2,5,64,256]{3,2,1,0:T(8,128)}, f32[2,256,128]{2,1,0:T(8,128)}, /*index...) while((s32[]{:T(128)}, f32[5]{0:T(128)S(1)}, ...), condition=%wide.region_19.20_spmd.clone.clone, body=%wide.region_7.19_spmd.clone.clone.sunk | while | flops 1212566272 | bytes 13529267 | solution.py:45
  276.7 3.9 fusion.227
  282.7 6.3 reduce-window.62
  290.2 1.9 fusion.240
  295.4 3.0 fusion.238
  299.9 3.9 fusion.227
  305.9 6.3 reduce-window.62
  318.6 3.0 fusion.238
  325.6 290.5 %all-reduce.8 = (f32[5]{0:T(128)}, f32[5]{0:T(128)}, bf16[320,2560]{0,1:T(8,128)(2,1)S(1)}) all-reduce(f32[5]{0:T(128)S(1)} %negate_multiply_fusion, f32[5]{0:T(128)S(1)} %reduce_sum.212, f32[320,2560]{0,1:T(8,128)} %fusion.127), channel_id=1, replica_groups=mesh['seq'=32,'dp'=2,'tensor'=8] {'seq','dp'}, use_global_device_ids=true, to_apply=%region_22.23 | all-reduce | flops 819210 | bytes 4915280 | tf_op jit(solution)/shard_map/psum | solution.py:114
  616.8 35.5 %all-reduce.9 = (bf16[512,128]{1,0:T(8,128)(2,1)}, bf16[512,128]{1,0:T(8,128)(2,1)}) all-reduce(f32[512,128]{1,0:T(8,128)S(1)} %bitcast.502, f32[512,128]{1,0:T(8,128)S(1)} %bitcast.503), channel_id=1, replica_groups=mesh['seq'=32,'dp'=2,'tensor'=8] {'tensor'}, use_global_device_ids=true, to_apply=%region_20.21 | all-reduce | flops 131072 | bytes 786432 | tf_op jit(solution)/shard_map/psum | solution.py:113
  (232 shorter events, 57.5 us)
Async XLA Ops:
  7.2 7.0 %copy-start.8 = (bf16[1,512,128]{2,1,0:T(8,128)(2,1)S(1)}, bf16[1,512,128]{2,1,0:T(8,128)(2,1)}, u32[]{:S(2)}) copy-start(bf16[1,512,128]{2,1,0:T(8,128)(2,1)} %param.13) | copy-start | bytes 393220
  7.2 25.5 %all-gather.9.cloned.1.call-start = ((), (), s32[]{:S(2)}) async-start(), calls=%async_computation | async-start | bytes 2457600 | tf_op jit(solution)/shard_map/all_gather | solution.py:86
  7.9 72.1 %all-gather.13.cloned.1.call-start = ((), (), s32[]{:S(2)}) async-start(), calls=%async_computation.2 | async-start | bytes 2949120 | tf_op jit(solution)/shard_map/all_gather | solution.py:84
  8.7 166.0 %all-gather.11.cloned.1.call-start = ((), (), s32[]{:S(2)}) async-start(), calls=%async_computation.1 | async-start | bytes 5406720 | tf_op jit(solution)/shard_map/all_gather | solution.py:71
  15.3 68.1 %copy-start.9 = (bf16[1,512,128]{2,1,0:T(8,128)(2,1)S(1)}, bf16[1,512,128]{2,1,0:T(8,128)(2,1)}, u32[]{:S(2)}) copy-start(bf16[1,512,128]{2,1,0:T(8,128)(2,1)} %param.14) | copy-start | bytes 393220
  15.3 69.2 %copy-start = (bf16[1,320,512]{2,1,0:T(8,128)(2,1)S(1)}, bf16[1,320,512]{2,1,0:T(8,128)(2,1)}, u32[]{:S(2)}) copy-start(bf16[1,320,512]{2,1,0:T(8,128)(2,1)} %param.12) | copy-start | bytes 983044
  15.3 250.2 %all-gather.15.cloned.1.call-start = ((), (), s32[]{:S(2)}) async-start(), calls=%async_computation.3 | async-start | bytes 5406720 | tf_op jit(solution)/shard_map/all_gather | solution.py:97
  83.3 83.7 %copy-start.3 = (bf16[320,512]{1,0:T(8,128)(2,1)}, bf16[320,512]{1,0:T(8,128)(2,1)S(1)}, u32[]{:S(2)}) copy-start(bf16[320,512]{1,0:T(8,128)(2,1)S(1)} %fusion.131) | copy-start | bytes 983044
  83.3 81.4 %copy-start.10 = (f32[1,5,512]{2,0,1:T(1,128)S(1)}, f32[1,5,512]{2,0,1:T(1,128)}, u32[]{:S(2)}) copy-start(f32[1,5,512]{2,0,1:T(1,128)} %param.15) | copy-start | bytes 30724
  83.3 81.6 %copy-start.11 = (f32[5]{0:T(128)S(1)}, f32[5]{0:T(128)}, u32[]{:S(2)}) copy-start(f32[5]{0:T(128)} %param.17) | copy-start | bytes 64
  191.2 3.7 copy-start.1
  194.9 0.8 copy-start.2
  202.8 3.6 copy-start.1
  206.4 0.8 copy-start.2
  211.3 5.4 copy-start.5
  322.0 1.7 copy-start.4
  322.0 2.7 copy-start.12
  323.8 293.0 %copy-start.6 = (f32[2,256,128]{2,1,0:T(8,128)S(1)}, f32[2,256,128]{2,1,0:T(8,128)}, u32[]{:S(2)}) copy-start(f32[2,256,128]{2,1,0:T(8,128)} %get-tuple-element.972) | copy-start | bytes 786436
  323.8 293.0 %copy-start.7 = (f32[2,256,128]{2,1,0:T(8,128)S(1)}, f32[2,256,128]{2,1,0:T(8,128)}, u32[]{:S(2)}) copy-start(f32[2,256,128]{2,1,0:T(8,128)} %get-tuple-element.973) | copy-start | bytes 786436
Sparse Core Ops, SparseCore 0:
  10.1 22.5 all-gather.8
  34.7 45.2 all-gather.12
  83.8 90.8 all-gather.10
  177.7 87.8 all-gather.14
where the time goes:
time: 660 us; the launch traced here: 659 us
  blocking collectives  403 us (61%)
  waiting for transfers between devices  121 us (18%)
  matrix products  63.7 us (10%)
  other arithmetic  33.6 us (5%)
  local copies, waits for them, and re-layouts  21.4 us (3%)
  between operations  15.6 us (2%)
    psum x1, blocking collectives, per_device(): grad_alog, grad_skip = lax.psum((grads[4], grads[5]), ('seq', 'dp'))  291 us
    unnamed x1, blocking collectives  76.9 us
    all_gather x1, waiting for transfers between devices, per_device(): shard_part = lax.all_gather(local_cotan[None], 'seq', axis=0, tiled=True)  48 us
    all_gather x1, waiting for transfers between devices, per_device(): g_full = lax.all_gather(out_grad[0], 'tensor', axis=0, tiled=True)  47.4 us
    psum x1, blocking collectives, per_device(): grad_b, grad_c = lax.psum((grads[1], grads[2]), 'tensor')  35.5 us
    dot_general x6, matrix products, span_pass(): block_out = jnp.einsum('hps,hts->hpt', x_block, scores, precision=HIGH)  18.5 us
    another operation x23, other arithmetic  17.6 us
    all_gather x1, waiting for transfers between devices, per_device(): lax.all_gather(w_out, 'dp', axis=1, tiled=True)  17.3 us
  transfers between devices with their start and end apart: 4, of which 4 were waited for; matrix products, arithmetic and copies ran while one was open for 9% of the time, Pallas kernels for 0%

commit v1 on v0

--- a/solution.py
+++ b/solution.py
@@ -111,7 +111,13 @@
         jnp.bfloat16
     )
     grad_b, grad_c = lax.psum((grads[1], grads[2]), "tensor")
-    grad_alog, grad_skip = lax.psum((grads[4], grads[5]), ("seq", "dp"))
+
+    def view_watch(vals):
+        for c in ("seq", "dp"):
+            vals = lax.psum(vals, c)
+        return vals
+
+    grad_alog, grad_skip = view_watch((grads[4], grads[5]))
     grad_inputs = grads[0].reshape(head_count * head_width, length).astype(jnp.bfloat16)
     return (
         mixed_half[None],

time: 660 us -> 691 us (1.047)
  the two profiles are of different devices: /device:TPU:16 before, /device:TPU:2 now
where the time goes in v1:
time: 691 us; the launch traced here: 690 us
  blocking collectives  482 us (70%)
  waiting for transfers between devices  71.8 us (10%)
  matrix products  63.8 us (9%)
  other arithmetic  33.7 us (5%)
  local copies, waits for them, and re-layouts  22.5 us (3%)
  between operations  15.5 us (2%)
    unnamed x2, blocking collectives  366 us
    psum x2, blocking collectives, view_watch(): vals = lax.psum(vals, c)  78.7 us
    all_gather x1, waiting for transfers between devices, per_device(): shard_part = lax.all_gather(local_state[None], 'seq', axis=0, tiled=True)  70.3 us
    psum x1, blocking collectives, per_device(): grad_b, grad_c = lax.psum((grads[1], grads[2]), 'tensor')  36.9 us
    dot_general x6, matrix products, span_pass(): block_out = jnp.einsum('hps,hts->hpt', x_block, scores, precision=HIGH)  18.5 us
    another operation x23, other arithmetic  17.6 us
  transfers between devices with their start and end apart: 4, of which 1 were waited for; matrix products, arithmetic and copies ran while one was open for 9% of the time, Pallas kernels for 0%

profile of v1, /device:TPU:2, one launch (start us, length us, event | category | flops | bytes accessed | tf_op | source)
XLA Modules:
  0.0 689.5 jit_solution(13781134656489730364)
XLA Ops:
  18.2 76.9 %all-reduce.2 = f32[160]{0:T(256)S(1)} all-reduce(f32[160]{0:T(256)S(1)} %dynamic-update-slice), channel_id=2, replica_groups=mesh['seq'=32,'dp'=2,'tensor'=8] {'seq'}, use_global_device_ids=true, to_apply=%add.2 | all-reduce | flops 160 | bytes 1280
  97.9 3.3 fusion.131
  103.2 70.3 %all-gather.11.cloned.1.call-done = f32[160,64,128]{2,1,0:T(8,128)} async-done(((f32[5,64,128]{2,1,0:T(8,128)}), f32[160,64,128]{2,1,0:T(8,128)}) %all-gather.11.cloned.1.call-update) | async-done | bytes 5242896 | tf_op jit(solution)/shard_map/all_gather | solution.py:71
  173.5 7.7 %fusion.125 = f32[5,1,64,128]{3,1,2,0:T(1,128)S(1)} fusion(f32[32,5,1,1]{0,2,3,1:T(1,128)S(1)} %copy.117, f32[32,5,64,128]{3,2,1,0:T(8,128)} %bitcast.487), kind=kOutput, calls=%fused_computation.159 | convolution fusion | flops 15728640 | bytes 5407360 | tf_op jit(solution)/shard_map/jh,jhpn->hpn/dot_general | solution.py:77
  184.0 23.3 %while.75 = (s32[]{:T(128)}, f32[5,64,128]{2,1,0:T(8,128)S(1)}, f32[2,5,64,256]{3,2,1,0:T(8,128)}, f32[2,5,256,256]{3,2,1,0:T(8,128)}, f32[2,128,256]{1,2,0:T(8,...) while((s32[]{:T(128)}, f32[5,64,128]{2,1,0:T(8,128)S(1)}, ...), condition=%wide.region_6.7_spmd.clone.clone, body=%wide.region_3.6_spmd.clone.clone.sunk | while | flops 607838976 | bytes 16159797 | solution.py:45
  187.1 2.9 multiply_dynamic-update-slice_fusion.4
  191.4 2.4 fusion.212
  198.8 2.8 multiply_dynamic-update-slice_fusion.4
  203.1 2.4 fusion.212
  210.3 5.3 fusion.127
  215.6 289.4 %all-reduce.10 = bf16[320,2560]{0,1:T(8,128)(2,1)} all-reduce(f32[320,2560]{0,1:T(8,128)} %fusion.127), channel_id=6, replica_groups=mesh['seq'=32,'dp'=2,'tensor'=8] {'seq','dp'}, use_global_device_ids=true, to_apply=%region_28.29.clone | all-reduce | flops 819200 | bytes 4915200
  507.3 7.7 %fusion.123 = f32[5,1,64,128]{3,1,2,0:T(1,128)S(1)} fusion(f32[32,5,1,1]{0,2,3,1:T(1,128)S(1)} %copy.120, f32[32,5,64,128]{3,2,1,0:T(8,128)} %bitcast.486), kind=kOutput, calls=%fused_computation.157 | convolution fusion | flops 15728640 | bytes 5407360 | tf_op jit(solution)/shard_map/jh,jhpn->hpn/dot_general | solution.py:105
  517.5 46.4 %while.76 = (s32[]{:T(128)}, f32[5]{0:T(128)S(1)}, f32[5,64,128]{2,1,0:T(8,128)S(1)}, f32[2,5,64,256]{3,2,1,0:T(8,128)}, f32[2,256,128]{2,1,0:T(8,128)}, /*index...) while((s32[]{:T(128)}, f32[5]{0:T(128)S(1)}, ...), condition=%wide.region_19.20_spmd.clone.clone, body=%wide.region_7.19_spmd.clone.clone.sunk | while | flops 1212566272 | bytes 13529267 | solution.py:45
  518.4 3.9 fusion.227
  524.5 6.3 reduce-window.62
  532.0 1.9 fusion.240
  537.2 3.0 fusion.238
  541.7 3.9 fusion.227
  547.7 6.3 reduce-window.62
  555.2 1.9 fusion.240
  560.4 3.0 fusion.238
  567.4 75.7 %all-reduce.4 = (f32[5]{0:T(128)S(1)}, f32[5]{0:T(128)S(1)}) all-reduce(f32[5]{0:T(128)S(1)} %negate_multiply_fusion, f32[5]{0:T(128)S(1)} %reduce_sum.212), channel_id=1, replica_groups=mesh['seq'=32,'dp'=2,'tensor'=8] {'seq'}, use_global_device_ids=true, to_apply=%region_22.23 | all-reduce | flops 10 | bytes 80 | tf_op jit(solution)/shard_map/psum | solution.py:117
  643.2 3.0 all-reduce.6
  646.1 36.9 %all-reduce.9 = (bf16[512,128]{1,0:T(8,128)(2,1)}, bf16[512,128]{1,0:T(8,128)(2,1)}) all-reduce(f32[512,128]{1,0:T(8,128)S(1)} %bitcast.502, f32[512,128]{1,0:T(8,128)S(1)} %bitcast.503), channel_id=1, replica_groups=mesh['seq'=32,'dp'=2,'tensor'=8] {'tensor'}, use_global_device_ids=true, to_apply=%region_20.21 | all-reduce | flops 131072 | bytes 786432 | tf_op jit(solution)/shard_map/psum | solution.py:113
  (234 shorter events, 56.7 us)
Async XLA Ops:
  7.2 8.3 %copy-start = (bf16[1,320,512]{2,1,0:T(8,128)(2,1)S(1)}, bf16[1,320,512]{2,1,0:T(8,128)(2,1)}, u32[]{:S(2)}) copy-start(bf16[1,320,512]{2,1,0:T(8,128)(2,1)} %param.12) | copy-start | bytes 983044
  7.2 7.1 %copy-start.8 = (bf16[1,512,128]{2,1,0:T(8,128)(2,1)S(1)}, bf16[1,512,128]{2,1,0:T(8,128)(2,1)}, u32[]{:S(2)}) copy-start(bf16[1,512,128]{2,1,0:T(8,128)(2,1)} %param.13) | copy-start | bytes 393220
  7.2 90.7 %all-gather.9.cloned.1.call-start = ((), (), s32[]{:S(2)}) async-start(), calls=%async_computation | async-start | bytes 2457600 | tf_op jit(solution)/shard_map/all_gather | solution.py:86
  7.9 90.0 %all-gather.13.cloned.1.call-start = ((), (), s32[]{:S(2)}) async-start(), calls=%async_computation.2 | async-start | bytes 2949120 | tf_op jit(solution)/shard_map/all_gather | solution.py:84
  8.7 164.9 %all-gather.11.cloned.1.call-start = ((), (), s32[]{:S(2)}) async-start(), calls=%async_computation.1 | async-start | bytes 5406720 | tf_op jit(solution)/shard_map/all_gather | solution.py:71
  13.1 82.4 %copy-start.9 = (bf16[1,512,128]{2,1,0:T(8,128)(2,1)S(1)}, bf16[1,512,128]{2,1,0:T(8,128)(2,1)}, u32[]{:S(2)}) copy-start(bf16[1,512,128]{2,1,0:T(8,128)(2,1)} %param.14) | copy-start | bytes 393220
  14.2 81.3 %copy-start.10 = (f32[1,5,512]{2,0,1:T(1,128)S(1)}, f32[1,5,512]{2,0,1:T(1,128)}, u32[]{:S(2)}) copy-start(f32[1,5,512]{2,0,1:T(1,128)} %param.15) | copy-start | bytes 30724
  14.2 81.5 %copy-start.11 = (f32[5]{0:T(128)S(1)}, f32[5]{0:T(128)}, u32[]{:S(2)}) copy-start(f32[5]{0:T(128)} %param.17) | copy-start | bytes 64
  15.4 491.9 %all-gather.15.cloned.1.call-start = ((), (), s32[]{:S(2)}) async-start(), calls=%async_computation.3 | async-start | bytes 5406720 | tf_op jit(solution)/shard_map/all_gather | solution.py:97
  101.2 0.7 copy-start.3
  190.2 3.7 copy-start.1
  193.9 0.8 copy-start.2
  201.8 3.6 copy-start.1
  205.5 0.8 copy-start.2
  215.6 290.8 %copy-start.5 = (f32[1,320,512]{2,1,0:T(8,128)S(1)}, f32[1,320,512]{2,1,0:T(8,128)}, u32[]{:S(2)}) copy-start(f32[1,320,512]{2,1,0:T(8,128)} %reshape.722) | copy-start | bytes 1966084
  563.8 1.8 copy-start.4
  563.9 2.7 copy-start.12
  563.9 82.3 %copy-start.6 = (f32[2,256,128]{2,1,0:T(8,128)S(1)}, f32[2,256,128]{2,1,0:T(8,128)}, u32[]{:S(2)}) copy-start(f32[2,256,128]{2,1,0:T(8,128)} %get-tuple-element.972) | copy-start | bytes 786436
  563.9 82.3 %copy-start.7 = (f32[2,256,128]{2,1,0:T(8,128)S(1)}, f32[2,256,128]{2,1,0:T(8,128)}, u32[]{:S(2)}) copy-start(f32[2,256,128]{2,1,0:T(8,128)} %get-tuple-element.973) | copy-start | bytes 786436
Sparse Core Ops, SparseCore 0:
  10.1 22.6 all-gather.8
  34.9 46.0 all-gather.12
  84.7 88.7 all-gather.10
  176.6 88.8 all-gather.14
